TPU v7x, 512 devices: a whole 4x8x8 slice. The times are simulated.
512 devices in a mesh: row: 16 (over x, y_lo, core), col: 32 (over z, y_hi).
Axes of the slice: x: 4, y: 8 (y_hi: 4, y_lo: 2; y = y_hi * 2 + y_lo), z: 8, core: 2. Of those that a mesh axis runs over, the one named last changes fastest.
Arguments:
- iterate: bfloat16 [8192, 4096], P('row', 'col'), may hold values from -0.125 to 0.125
Outputs:
- update: bfloat16 [8192, 4096], P('row', 'col')
All inputs are finite; a program needn't handle non-finite values.
Results may differ from a plain program's by a relative error of at most 0.0068.
Values may be sent and summed in bfloat16 or wider, within the bound.
A program may use at most 64 MiB of HBM per device.

v0:
```python
import math

import jax
import jax.numpy as jnp
from jax import lax
from jax.sharding import PartitionSpec as P


def from_root(block, axis, owner):
    block = jnp.where(lax.axis_index(axis) == owner, block, jnp.zeros_like(block))
    return lax.psum(block, axis)


def left_product(left_side, right_side):
    return lax.dot_general(
        left_side, right_side, (((0,), (0,)), ((), ())), preferred_element_type=jnp.float32
    )


def body(iterate):
    local_rows, local_cols = iterate.shape
    row_count = lax.axis_size("row")
    col_count = lax.axis_size("col")
    total_rows = local_rows * row_count
    total_cols = local_cols * col_count
    column_stripe = lax.all_gather(iterate, "row", axis=0, tiled=True)
    groups = col_count // row_count
    mirrored = []
    for offset in range(groups):
        mirrored.append(from_root(column_stripe, "col", groups * lax.axis_index("row") + offset))
    gram_block = left_product(jnp.concatenate(mirrored, axis=1), column_stripe)
    gram_half = gram_block.astype(jnp.bfloat16)
    gram_columns = lax.all_gather(gram_half, "row", axis=0, tiled=True)

    def add_rows(segment):
        return jnp.dot(segment, gram_columns, preferred_element_type=jnp.float32)

    first_term = add_rows(lax.all_gather(iterate, "col", axis=1, tiled=True))
    first_half = first_term.astype(jnp.bfloat16)
    second_term = add_rows(lax.all_gather(first_half, "col", axis=1, tiled=True))
    update_scale = 0.2 * math.sqrt(max(total_rows, total_cols))
    mixed = 3.4445 * iterate.astype(jnp.float32) - 4.775 * first_term + 2.0315 * second_term
    return (update_scale * mixed).astype(jnp.bfloat16)


def solution(mesh):
    placed = (P("row", "col"),)
    return jax.shard_map(
        body, mesh=mesh, in_specs=placed, out_specs=P("row", "col"), check_vma=False
    )
```

profile of v0, /device:TPU:1, one launch (start us, length us, event | category | flops | bytes accessed | tf_op | source)
XLA Modules:
  0.0 660.9 jit_solution(11465887851437480017)
XLA Ops:
  6.5 0.7 all-gather.5.cloned.1.call-update
  7.3 0.0 all-reduce.3.cloned.1.call-start
  7.3 47.4 %all-gather.5.cloned.1.call-done = bf16[8192,128]{1,0:T(8,128)(2,1)} async-done(((bf16[512,128]{1,0:T(8,128)(2,1)}), bf16[8192,128]{1,0:T(8,128)(2,1)}) %all-gather.5.cloned.1.call-update) | async-done | bytes 2097168 | tf_op jit(solution)/shard_map/all_gather | solution.py:26
  54.8 3.9 broadcast_select_fusion.1
  58.7 0.0 all-reduce.3.cloned.1.call-update
  58.7 0.0 all-gather.9.cloned.1.call-start
  58.8 0.7 all-gather.9.cloned.1.call-update
  59.5 0.0 all-gather.7.cloned.1.call-start
  59.5 329.5 %all-reduce.3.cloned.1.call-done = (bf16[8192,128]{1,0:T(8,128)(2,1)}, bf16[8192,128]{1,0:T(8,128)(2,1)}) async-done(((bf16[8192,128]{1,0:T(8,128)(2,1)}, bf16[8192,128]{1,0:T(8,128)(2,1)}), (bf16[8192,128]{1,0:T(8,128)(2,1)}, bf16[8192,128]{1,0:T(8,128)(2,1)})) %all-reduce.3.cloned.1.call-update) | async-done | bytes 4194320 | tf_op jit(solution)/shard_map/psum | solution.py:11
  389.0 4.2 fusion.7
  393.1 0.0 all-gather.7.cloned.1.call-update
  393.1 0.0 copy-start.1
  393.2 0.0 all-gather.11.cloned.1.call-start
  393.2 112.0 %all-gather.9.cloned.1.call-done = bf16[512,4096]{1,0:T(8,128)(2,1)} async-done(((bf16[512,128]{1,0:T(8,128)(2,1)}), bf16[512,4096]{1,0:T(8,128)(2,1)}) %all-gather.9.cloned.1.call-update) | async-done | bytes 4194320 | tf_op jit(solution)/shard_map/all_gather | solution.py:38
  505.2 40.1 %all-gather.7.cloned.1.call-done = bf16[4096,128]{1,0:T(8,128)(2,1)} async-done(((bf16[256,128]{1,0:T(8,128)(2,1)}), bf16[4096,128]{1,0:T(8,128)(2,1)}) %all-gather.7.cloned.1.call-update) | async-done | bytes 1048592 | tf_op jit(solution)/shard_map/all_gather | solution.py:33
  545.3 4.1 fusion.11
  549.5 0.7 convert_bitcast_fusion
  550.1 0.0 all-gather.11.cloned.1.call-update
  550.2 0.0 copy-done.1
  550.2 0.1 copy.2
  550.3 100.4 %all-gather.11.cloned.1.call-done = bf16[512,4096]{0,1:T(8,128)(2,1)} async-done(((bf16[512,128]{0,1:T(8,128)(2,1)}), bf16[512,4096]{0,1:T(8,128)(2,1)}) %all-gather.11.cloned.1.call-update) | async-done | bytes 4194320 | tf_op jit(solution)/shard_map/all_gather | solution.py:40
  650.6 0.0 copy-done.2
  650.6 3.0 fusion.6
  653.6 0.8 copy.4
  (4 shorter events, 0.0 us)
Async XLA Ops:
  6.5 48.2 %all-gather.5.cloned.1.call-start = ((), (), s32[]{:S(2)}) async-start(), calls=%async_computation | async-start | bytes 2228224 | tf_op jit(solution)/shard_map/all_gather | solution.py:26
  7.3 381.7 %all-reduce.3.cloned.1.call-start = ((), (), s32[]{:S(2)}) async-start(), calls=%async_computation.4 | async-start | bytes 8388608 | tf_op jit(solution)/shard_map/psum | solution.py:11
  58.7 330.3 %copy-start = (bf16[8192,128]{1,0:T(8,128)(2,1)S(1)}, bf16[8192,128]{1,0:T(8,128)(2,1)}, u32[]{:S(2)}) copy-start(bf16[8192,128]{1,0:T(8,128)(2,1)} %all-gather.5.cloned.1.call-done) | copy-start | bytes 6291460
  58.7 446.5 %all-gather.9.cloned.1.call-start = ((), (), s32[]{:S(2)}) async-start(), calls=%async_computation.2 | async-start | bytes 4325376 | tf_op jit(solution)/shard_map/all_gather | solution.py:38
  59.5 485.9 %all-gather.7.cloned.1.call-start = ((), (), s32[]{:S(2)}) async-start(), calls=%async_computation.1 | async-start | bytes 1114112 | tf_op jit(solution)/shard_map/all_gather | solution.py:33
  393.1 157.0 %copy-start.1 = (bf16[512,128]{1,0:T(8,128)(2,1)S(1)}, bf16[512,128]{1,0:T(8,128)(2,1)}, u32[]{:S(2)}) copy-start(bf16[512,128]{1,0:T(8,128)(2,1)} %param.1) | copy-start | bytes 393220
  393.2 257.5 %all-gather.11.cloned.1.call-start = ((), (), s32[]{:S(2)}) async-start(), calls=%async_computation.3 | async-start | bytes 4325376 | tf_op jit(solution)/shard_map/all_gather | solution.py:40
  545.3 105.3 %copy-start.2 = (bf16[4096,128]{1,0:T(8,128)(2,1)S(1)}, bf16[4096,128]{1,0:T(8,128)(2,1)}, u32[]{:S(2)}) copy-start(bf16[4096,128]{1,0:T(8,128)(2,1)} %all-gather.7.cloned.1.call-done) | copy-start | bytes 3145732
Sparse Core Ops, SparseCore 0:
  9.5 45.2 all-gather.4
  58.8 330.0 all-reduce.2
  392.0 113.1 all-gather.8
  507.2 38.0 all-gather.6
  550.3 100.3 all-gather.10
where the time goes:
time: 663 us; the launch traced here: 661 us
  waiting for transfers between devices  631 us (95%)
  between operations  13.2 us (2%)
  matrix products  11.2 us (2%)
    psum x1, waiting for transfers between devices, from_root(): return lax.psum(block, axis)  329 us
    all_gather x1, waiting for transfers between devices, body(): first_term = add_rows(lax.all_gather(iterate, 'col', axis=1, tiled=True))  112 us
    all_gather x1, waiting for transfers between devices, body(): lax.all_gather(first_half, 'col', axis=1, tiled=True)  100 us
    all_gather x1, waiting for transfers between devices, body(): column_stripe = lax.all_gather(iterate, 'row', axis=0, tiled=True)  47.4 us
    all_gather x1, waiting for transfers between devices, body(): gram_columns = lax.all_gather(gram_half, 'row', axis=0, tiled=True)  40.1 us
  transfers between devices with their start and end apart: 5, of which 5 were waited for; matrix products, arithmetic and copies ran while one was open for 1% of the time, Pallas kernels for 0%

commit v1 on v0

v1 whole, which is shorter than its diff:
```python
import math

import jax
import jax.numpy as jnp
from jax import lax
from jax.experimental import pallas as pl
from jax.experimental.pallas import tpu as pltpu
from jax.sharding import PartitionSpec as P

MESH = pl.DeviceIdType.MESH
BF16 = jnp.bfloat16
F32 = jnp.float32

R, W = 512, 128
NZ, NY = 8, 4
GATHER_CHUNKS = 2
ROW_CHUNKS = 4
SLABS = [(dx, dy) for dx in range(4) for dy in range(2) if (dx, dy) != (0, 0)]
SCALE = 0.2 * math.sqrt(8192)


class Copies:
    def __init__(self, send_sems, recv_sems):
        self.send_sems, self.recv_sems, self.used, self.started = send_sems, recv_sems, 0, []

    def make(self, src, dst, device):
        at = self.used
        self.used += 1
        return pltpu.make_async_remote_copy(
            src_ref=src,
            dst_ref=dst,
            send_sem=self.send_sems.at[at],
            recv_sem=self.recv_sems.at[at],
            device_id=device,
            device_id_type=MESH,
        )

    def start(self, src, dst, device):
        copy = self.make(src, dst, device)
        copy.start()
        self.started.append(copy)
        return copy


def tdot(left, right):
    return lax.dot_general(left, right, (((0,), (0,)), ((), ())), preferred_element_type=F32)


def ring_plan(chunks):
    order = []
    for t in range(1, 5 + chunks):
        for c in range(chunks):
            k = t - c
            if 1 <= k <= 3:
                order += [(k, c), (NZ - k, c)]
            elif k == 4:
                order.append((4, c))
    return order


def kernel(x_ref, o_ref, xa, xb, xao, xbo, gp, rb, g, sa, ra, sb, rbb, ah, acc, send_sems, recv_sems):
    r, c_ = lax.axis_index("row"), lax.axis_index("col")
    x, yl, q = r // 4, (r // 2) % 2, r % 2
    z, yh = c_ // 4, c_ % 4
    slab = x * 2 + yl
    sibling = (x * 4 + yl * 2 + (1 - q), c_)
    z_up = (r, ((z + 1) % NZ) * 4 + yh)
    z_down = (r, ((z + NZ - 1) % NZ) * 4 + yh)
    y_dev = {e: (r, z * 4 + (yh + e) % NY) for e in range(1, NY)}
    slab_of = {}
    slab_dev = {}
    slab_from = {}
    for dx, dy in SLABS:
        tx, ty = (x + dx) % 4, (yl + dy) % 2
        slab_of[dx, dy] = tx * 2 + ty
        slab_dev[dx, dy] = (tx * 4 + ty * 2 + q, c_)
        slab_from[dx, dy] = ((x + 4 - dx) % 4) * 2 + (yl + dy) % 2

    barrier = pltpu.get_barrier_semaphore()
    partners = [sibling, z_up, z_down] + list(y_dev.values()) + list(slab_dev.values())
    for device in partners:
        pl.semaphore_signal(barrier, inc=1, device_id=device, device_id_type=MESH)
    pl.semaphore_wait(barrier, len(partners))

    cps = Copies(send_sems, recv_sems)

    def cols(ref, at, rows=None):
        return ref.at[:, pl.ds(at * W, W)] if rows is None else ref.at[rows, pl.ds(at * W, W)]

    def chunk_rows(c, chunks):
        return pl.ds(c * (R // chunks), R // chunks)

    def forward(buf, k, c, chunks, first=None):
        rows = chunk_rows(c, chunks)
        src = cols(buf, k, rows) if first is None else first.at[rows, :]
        got = []
        if k <= 3 and (k < 3 or c % 2 == 0):
            got.append((k + 1, c, cps.start(src, cols(buf, k + 1, rows), z_down)))
        if (k == 0 or k >= 5) and (k != 5 or c % 2 == 1):
            m = (k + NZ - 1) % NZ
            got.append((m, c, cps.start(src, cols(buf, m, rows), z_up)))
        return got

    arrive = {}
    for c in range(GATHER_CHUNKS):
        for k, cc, copy in forward(xa, 0, c, GATHER_CHUNKS, x_ref):
            arrive[k, cc] = copy
    y_in = {}
    for e in (1, 3, 2):
        y_in[NY - e] = cps.start(x_ref, cols(xb, NY - e), y_dev[e])
    sib_in = [cps.start(x_ref, cols(xbo, 0), sibling)]
    xa[:, 0:W] = x_ref[...]
    xb[:, 0:W] = x_ref[...]

    half_in = []

    def to_sibling(k, c):
        rows = chunk_rows(c, GATHER_CHUNKS)
        copy = cps.make(cols(xa, k, rows), cols(xao, k % 4, rows), sibling)
        half_in.append((k // 4, copy))

        @pl.when(q != k // 4)
        def _():
            copy.start()

    for c in range(GATHER_CHUNKS):
        to_sibling(0, c)
    order = ring_plan(GATHER_CHUNKS)
    for n, (k, c) in enumerate(order):
        arrive[k, c].wait_recv()
        for kk, cc, copy in forward(xa, k, c, GATHER_CHUNKS) if k != 4 else []:
            arrive[kk, cc] = copy
        to_sibling(k, c)
    for e in (1, 3, 2):
        y_in[e].wait_recv()
        sib_in.append(cps.start(cols(xb, e), cols(xbo, e), sibling))
    for copy in sib_in:
        copy.wait_recv()
    for owner, copy in half_in:

        @pl.when(q == owner)
        def _(copy=copy):
            copy.wait_recv()

    for i in range(4):
        at = pl.multiple_of(q * (4 * W) + i * W, W)
        part = tdot(xa[:, pl.ds(at, W)], xb[...])
        part += tdot(xao[:, i * W : (i + 1) * W], xbo[...])
        half = part.astype(BF16)
        gp[2 * i] = half[:64]
        gp[2 * i + 1] = half[64:]

    rs_in = []
    for j, d in enumerate(SLABS):
        rs_in.append(cps.start(gp.at[slab_of[d]], rb.at[j], slab_dev[d]))
    total = gp[slab].astype(F32)
    for j, copy in enumerate(rs_in):
        copy.wait_recv()
        total += rb[j].astype(F32)
    half_rows = q * (4 * W)

    def piece(w):
        return g.at[pl.ds(pl.multiple_of(half_rows + w * 64, 64), 64), :]

    piece(slab)[...] = total.astype(BF16)
    ag_in = []
    for d in SLABS:
        ag_in.append((d, cps.start(piece(slab), piece(slab), slab_dev[d])))
    g_in = [cps.start(piece(slab), piece(slab), sibling)]
    for d, copy in ag_in:
        copy.wait_recv()
        g_in.append(cps.start(piece(slab_from[d]), piece(slab_from[d]), sibling))
    for copy in g_in:
        copy.wait_recv()

    RC = R // ROW_CHUNKS
    a_in = {}
    for c in range(ROW_CHUNKS):
        rows = pl.ds(c * RC, RC)
        part = jnp.dot(xa[rows, :], g[...], preferred_element_type=F32)
        acc[rows, :] = part[:, :W]
        for e in (1, 3, 2):
            sa[rows, e * W : (e + 1) * W] = part[:, e * W : (e + 1) * W].astype(BF16)
            a_in[NY - e, c] = cps.start(cols(sa, e, rows), cols(ra, NY - e, rows), y_dev[e])

    a_arrive, b_in = {}, {}

    def finish_first(c):
        rows = pl.ds(c * RC, RC)
        first = acc[rows, :]
        for e in (1, 3, 2):
            a_in[e, c].wait_recv()
            first += ra[rows, e * W : (e + 1) * W].astype(F32)
        acc[rows, :] = first
        ah[rows, 0:W] = first.astype(BF16)
        for k, cc, copy in forward(ah, 0, c, ROW_CHUNKS):
            a_arrive[k, cc] = copy

    def second_product(c):
        rows = pl.ds(c * RC, RC)
        part = jnp.dot(ah[rows, :], g[...], preferred_element_type=F32)
        for e in (1, 3, 2):
            sb[rows, e * W : (e + 1) * W] = part[:, e * W : (e + 1) * W].astype(BF16)
            b_in[NY - e, c] = cps.start(
                cols(sb, e, rows), cols(rbb, NY - e, rows), y_dev[e]
            )
        mixed = 3.4445 * x_ref[rows, :].astype(F32) - 4.775 * acc[rows, :]
        acc[rows, :] = mixed + 2.0315 * part[:, :W]

    for t in range(ROW_CHUNKS + 5):
        for c in range(ROW_CHUNKS):
            k = t - c
            if k == 0:
                finish_first(c)
            for kk in {1: (1, 7), 2: (2, 6), 3: (3, 5), 4: (4,)}.get(k, ()):
                a_arrive[kk, c].wait_recv()
                for k2, c2, copy in forward(ah, kk, c, ROW_CHUNKS) if kk != 4 else []:
                    a_arrive[k2, c2] = copy
            if k == 4:
                second_product(c)

    for c in range(ROW_CHUNKS):
        rows = pl.ds(c * RC, RC)
        second = jnp.zeros((RC, W), F32)
        for e in (1, 3, 2):
            b_in[e, c].wait_recv()
            second += rbb[rows, e * W : (e + 1) * W].astype(F32)
        o_ref[rows, :] = (SCALE * (acc[rows, :] + 2.0315 * second)).astype(BF16)

    for copy in cps.started:
        copy.wait_send()
    for owner, copy in half_in:

        @pl.when(q != owner)
        def _(copy=copy):
            copy.wait_send()


COPIES = 160


def body(iterate):
    vmem = pl.BlockSpec(memory_space=pltpu.VMEM)
    return pl.pallas_call(
        kernel,
        out_shape=jax.ShapeDtypeStruct((R, W), BF16),
        in_specs=[vmem],
        out_specs=vmem,
        scratch_shapes=[
            pltpu.VMEM((R, NZ * W), BF16),
            pltpu.VMEM((R, NY * W), BF16),
            pltpu.VMEM((R, 4 * W), BF16),
            pltpu.VMEM((R, NY * W), BF16),
            pltpu.VMEM((8, 64, NY * W), BF16),
            pltpu.VMEM((7, 64, NY * W), BF16),
            pltpu.VMEM((NZ * W, NY * W), BF16),
            pltpu.VMEM((R, NY * W), BF16),
            pltpu.VMEM((R, NY * W), BF16),
            pltpu.VMEM((R, NY * W), BF16),
            pltpu.VMEM((R, NY * W), BF16),
            pltpu.VMEM((R, NZ * W), BF16),
            pltpu.VMEM((R, W), F32),
            pltpu.SemaphoreType.DMA((COPIES,)),
            pltpu.SemaphoreType.DMA((COPIES,)),
        ],
        compiler_params=pltpu.CompilerParams(
            collective_id=0, has_side_effects=True, vmem_limit_bytes=32 << 20
        ),
        name="newton_schulz",
    )(iterate)


def solution(mesh):
    placed = (P("row", "col"),)
    return jax.shard_map(
        body, mesh=mesh, in_specs=placed, out_specs=P("row", "col"), check_vma=False
    )
```

time: 663 us -> 97.6 us (0.15)
  the two profiles are of different devices: /device:TPU:1 before, /device:TPU:8 now
where the time goes in v1:
time: 97.6 us; the launch traced here: 97.5 us
  Pallas kernels  95.9 us (98%)
  local copies, waits for them, and re-layouts  1.56 us (2%)
    pallas_call x1, Pallas kernels, body(): pl.pallas_call(kernel, out_shape=jax.ShapeDtypeStruct((R, W), BF16), in_s...  95.9 us

profile of v1, /device:TPU:8, one launch (start us, length us, event | category | flops | bytes accessed | tf_op | source)
XLA Modules:
  0.0 97.5 jit_solution(1583912499790938600)
XLA Ops:
  0.0 0.0 copy-start
  0.0 0.9 copy-done
  0.9 95.9 %newton_schulz.1 = bf16[512,128]{1,0:T(8,128)(2,1)S(1)} custom-call(bf16[512,128]{1,0:T(8,128)(2,1)S(1)} %copy-done), custom_call_target="tpu_custom_call" | custom-call | tf_op jit(solution)/shard_map/newton_schulz/pallas_call | solution.py:244
  96.8 0.7 copy.3
Async XLA Ops:
  0.0 0.9 copy-start

commit v2 on v0

v2 whole, which is shorter than its diff:
```python
import math

import jax
import jax.numpy as jnp
from jax import lax
from jax.experimental import pallas as pl
from jax.experimental.pallas import tpu as pltpu
from jax.sharding import PartitionSpec as P

MESH = pl.DeviceIdType.MESH
BF16 = jnp.bfloat16
F32 = jnp.float32

R, W = 512, 128
NZ, NY = 8, 4
U = 256
V = R - U
PARTS = 2
SLABS = [(dx, dy) for dx in (2, 1, 3, 0) for dy in (1, 0) if (dx, dy) != (0, 0)]
SCALE = 0.2 * math.sqrt(8192)
PLACE = {d: i for i, d in enumerate((0, 1, 7, 2, 6, 3, 5, 4))}
GRAM_CHUNKS = ((0, 5), (5, 8))


def tdot(left, right):
    return lax.dot_general(left, right, (((0,), (0,)), ((), ())), preferred_element_type=F32)


def kernel(
    x_hbm, o_ref, x_ref, xa, xb, xao, xbo, gp, rb, g, su1, ru1, su2, ru2, ov1, rv1, fv1, ov2, rv2, fv2, ah, av, kept, through, acc,
    load_sem, send_sems, recv_sems,
):
    r, c_ = lax.axis_index("row"), lax.axis_index("col")
    x, yl, q = r // 4, (r // 2) % 2, r % 2
    z, yh = c_ // 4, c_ % 4
    slab = x * 2 + yl
    sibling = (x * 4 + yl * 2 + (1 - q), c_)
    z_dev = {d: (r, ((z + d) % NZ) * 4 + yh) for d in (1, 2, 6, 7)}
    y_dev = {e: (r, z * 4 + (yh + e) % NY) for e in range(1, NY)}
    slab_of, slab_dev, slab_from = {}, {}, {}
    for dx, dy in SLABS:
        tx, ty = (x + dx) % 4, (yl + dy) % 2
        slab_of[dx, dy] = tx * 2 + ty
        slab_dev[dx, dy] = (tx * 4 + ty * 2 + q, c_)
        slab_from[dx, dy] = ((x + 4 - dx) % 4) * 2 + ty

    load = pltpu.make_async_copy(x_hbm, x_ref, load_sem)
    load.start()
    barrier = pltpu.get_barrier_semaphore()
    partners = [sibling] + list(z_dev.values()) + list(y_dev.values()) + list(slab_dev.values())
    for device in partners:
        pl.semaphore_signal(barrier, inc=1, device_id=device, device_id_type=MESH)
    load.wait()
    xa[:, 0:W] = x_ref[...]
    xb[:, 0:W] = x_ref[...]
    pl.semaphore_wait(barrier, len(partners))

    started = []

    def send(src, dst, device):
        at = len(started)
        copy = pltpu.make_async_remote_copy(
            src_ref=src,
            dst_ref=dst,
            send_sem=send_sems.at[at],
            recv_sem=recv_sems.at[at],
            device_id=device,
            device_id_type=MESH,
        )
        copy.start()
        started.append(copy)
        return copy

    def slot(ref, at, first=0, count=R):
        return ref.at[pl.ds(first, count), pl.ds(at * W, W)]

    def z_near(src, buf, first, count):
        got = {}
        for d in (2, 6, 1, 7):
            got[(NZ - d) % NZ] = send(src, slot(buf, PLACE[(NZ - d) % NZ], first, count), z_dev[d])
        return got

    def z_far(buf, d, first, count, got):
        step = 7 if d == 2 else 1
        twice = 6 if d == 2 else 2
        far = 3 if d == 2 else 5
        here = slot(buf, PLACE[d], first, count)
        got[far] = send(here, slot(buf, PLACE[far], first, count), z_dev[step])
        half = first if d == 2 else first + count // 2
        got[4, d] = send(
            slot(buf, PLACE[d], half, count // 2), slot(buf, PLACE[4], half, count // 2), z_dev[twice]
        )

    z_in = {}
    PART = R // PARTS
    for near in ((2, 6), (1, 7)):
        for p in range(PARTS):
            for d in near:
                src = x_ref.at[pl.ds(p * PART, PART), :]
                z_in[NZ - d, p] = send(src, slot(xa, PLACE[NZ - d], p * PART, PART), z_dev[d])
    y_in = {NY - e: send(x_ref, slot(xb, NY - e), y_dev[e]) for e in (2, 1, 3)}
    xa_in = {0: send(x_ref, slot(xao, 0), sibling)}
    xb_in = {0: send(x_ref, slot(xbo, 0), sibling)}

    def pass_xa(d):
        xa_in[d] = send(slot(xa, PLACE[d]), slot(xao, PLACE[d]), sibling)

    far_in = [{} for _ in range(PARTS)]
    for p in range(PARTS):
        for d in (2, 6):
            z_in[d, p].wait_recv()
            z_far(xa, d, p * PART, PART, far_in[p])
    pass_xa(2)
    pass_xa(6)
    for d in (1, 7):
        for p in range(PARTS):
            z_in[d, p].wait_recv()
        pass_xa(d)
    for e in (1, 3, 2):
        y_in[e].wait_recv()
        xb_in[e] = send(slot(xb, e), slot(xbo, e), sibling)
    for e in (0, 1, 3, 2):
        xb_in[e].wait_recv()

    own = pl.ds(pl.multiple_of(q * (2 * W), 2 * W), 2 * W)

    def gram_rows(chunk):
        first, last = GRAM_CHUNKS[chunk]
        for at in range(first, last):
            part = tdot(xa[:, at * W : (at + 1) * W], xb[:, own])
            part += tdot(xao[:, at * W : (at + 1) * W], xbo[:, own])
            gp[at * W : (at + 1) * W, :] = part.astype(BF16)

    def piece(chunk, w):
        first, last = GRAM_CHUNKS[chunk]
        rows = (last - first) * (W // 8)
        return pl.ds(pl.multiple_of(first * W + w * rows, 16), rows)

    def reduce_start(chunk):
        first, last = GRAM_CHUNKS[chunk]
        rows = (last - first) * (W // 8)
        got = []
        for j, d in enumerate(SLABS):
            dst = rb.at[j, pl.ds(first * (W // 8), rows), :]
            got.append((j, send(gp.at[piece(chunk, slab_of[d]), :], dst, slab_dev[d])))
        return got

    def reduce_finish(chunk, got):
        first, last = GRAM_CHUNKS[chunk]
        mine = piece(chunk, slab)
        total = gp[mine, :].astype(F32)
        for j, copy in got:
            copy.wait_recv()
            total += rb[j, first * (W // 8) : last * (W // 8), :].astype(F32)
        g[mine, own] = total.astype(BF16)
        here = g.at[mine, own]
        gather = [(piece(chunk, slab_from[d]), send(here, here, slab_dev[d])) for d in SLABS]
        return gather, [send(here, here, sibling)]

    def gather_finish(gather, both):
        for rows, copy in gather:
            copy.wait_recv()
            here = g.at[rows, own]
            both.append(send(here, here, sibling))

    for d in (0, 2, 6, 1, 7):
        xa_in[d].wait_recv()
    gram_rows(0)
    reduce_0 = reduce_start(0)
    for d in (3, 5):
        for p in range(PARTS):
            far_in[p][d].wait_recv()
        pass_xa(d)
    for p in range(PARTS):
        for d in (2, 6):
            far_in[p][4, d].wait_recv()
    pass_xa(4)
    for d in (3, 5, 4):
        xa_in[d].wait_recv()
    gram_rows(1)
    reduce_1 = reduce_start(1)
    gather_0, both_0 = reduce_finish(0, reduce_0)
    gather_1, both_1 = reduce_finish(1, reduce_1)
    gather_finish(gather_0, both_0)
    gather_finish(gather_1, both_1)
    for copy in both_0 + both_1:
        copy.wait_recv()

    def u_product(rows_of, out, into):
        got = {}
        high = jnp.dot(rows_of[:U, :], g[:, 2 * W :], preferred_element_type=F32).astype(BF16)
        for e in (2, 3):
            out[:, e * W : (e + 1) * W] = high[:, (e - 2) * W : (e - 1) * W]
            got[NY - e] = send(slot(out, e, 0, U), slot(into, NY - e, 0, U), y_dev[e])
        low = jnp.dot(rows_of[:U, :], g[:, : 2 * W], preferred_element_type=F32)
        out[:, W : 2 * W] = low[:, W:].astype(BF16)
        got[3] = send(slot(out, 1, 0, U), slot(into, 3, 0, U), y_dev[1])
        return low[:, :W], got

    def u_sum(total, into, got):
        for e in (1, 3, 2):
            got[e].wait_recv()
            total += into[:, e * W : (e + 1) * W].astype(F32)
        return total

    def v_product(left, out, relay, into):
        part = lax.dot_general(
            left, g[...], (((1,), (1,)), ((), ())), preferred_element_type=F32
        )
        out[...] = part.astype(BF16)
        got = {}
        half = V // 2
        for n, d, first in ((2, 2, 0), (3, 6, half)):
            got[n] = send(slot(out, PLACE[4], first, half), relay.at[n, pl.ds(0, half), :], z_dev[d])
        for n, d, far in ((0, 1, 3), (1, 7, 5)):
            got[n] = send(slot(out, PLACE[far], 0, V), relay.at[n], z_dev[d])
        near = [send(slot(out, PLACE[d], 0, V), into.at[n], z_dev[d]) for n, d in ((0, 1), (1, 7))]
        for n, d in ((0, 2), (1, 6)):
            kept[n] = part[:, PLACE[d] * W : (PLACE[d] + 1) * W]
        return part[:, :W], got, near

    def v_relay(stage, relay, into, got, near):
        half = V // 2
        for n, d in ((0, 2), (1, 6)):
            got[n].wait_recv()
            total = kept[n] + relay[n].astype(F32)
            got[n + 2].wait_recv()
            more = relay[n + 2, :half, :].astype(F32)
            through[stage, n, :half] = (total[:half] + more if n == 0 else total[:half]).astype(BF16)
            through[stage, n, half:] = (total[half:] + more if n == 1 else total[half:]).astype(BF16)
            near.append(send(through.at[stage, n], into.at[n + 2], z_dev[d]))

    def v_sum(total, into, near):
        for n, copy in enumerate(near):
            copy.wait_recv()
            total += into[n].astype(F32)
        return total

    def mix(rows, first):
        return 3.4445 * x_ref[rows, :].astype(F32) - 4.775 * first

    urows, vrows = slice(0, U), slice(U, R)
    v_own, v_far, v_near = v_product(xb[vrows, :], ov1, rv1, fv1)
    acc[vrows, :] = v_own
    u_own, u_in = u_product(xa, su1, ru1)
    acc[urows, :] = u_own

    v_relay(0, rv1, fv1, v_far, v_near)
    first = u_sum(acc[urows, :], ru1, u_in)
    ah[:, 0:W] = first.astype(BF16)
    ah_in = z_near(slot(ah, 0, 0, U), ah, 0, U)
    acc[urows, :] = mix(urows, first)
    first = v_sum(acc[vrows, :], fv1, v_near)
    av[:, 0:W] = first.astype(BF16)
    av_in = [send(slot(av, 0, 0, V), slot(av, NY - e, 0, V), y_dev[e]) for e in (2, 1, 3)]
    acc[vrows, :] = mix(vrows, first)
    for d in (2, 6):
        ah_in[d].wait_recv()
        z_far(ah, d, 0, U, ah_in)
    for copy in av_in:
        copy.wait_recv()
    v_own, v_far, v_near = v_product(av[...], ov2, rv2, fv2)
    acc[vrows, :] += 2.0315 * v_own
    for d in (1, 7, 3, 5, (4, 2), (4, 6)):
        ah_in[d].wait_recv()
    u_own, u_in = u_product(ah, su2, ru2)
    acc[urows, :] += 2.0315 * u_own
    v_relay(1, rv2, fv2, v_far, v_near)
    second = u_sum(jnp.zeros((U, W), F32), ru2, u_in)
    o_ref[urows, :] = (SCALE * (acc[urows, :] + 2.0315 * second)).astype(BF16)
    second = v_sum(jnp.zeros((V, W), F32), fv2, v_near)
    o_ref[vrows, :] = (SCALE * (acc[vrows, :] + 2.0315 * second)).astype(BF16)

    for copy in started:
        copy.wait_send()


COPIES = 128


def body(iterate):
    return pl.pallas_call(
        kernel,
        out_shape=jax.ShapeDtypeStruct((R, W), BF16),
        in_specs=[pl.BlockSpec(memory_space=pl.ANY)],
        out_specs=pl.BlockSpec(memory_space=pltpu.VMEM),
        scratch_shapes=[
            pltpu.VMEM((R, W), BF16),
            pltpu.VMEM((R, NZ * W), BF16),
            pltpu.VMEM((R, NY * W), BF16),
            pltpu.VMEM((R, NZ * W), BF16),
            pltpu.VMEM((R, NY * W), BF16),
            pltpu.VMEM((NZ * W, 2 * W), BF16),
            pltpu.VMEM((7, NZ * W // 8, 2 * W), BF16),
            pltpu.VMEM((NZ * W, NY * W), BF16),
            pltpu.VMEM((U, NY * W), BF16),
            pltpu.VMEM((U, NY * W), BF16),
            pltpu.VMEM((U, NY * W), BF16),
            pltpu.VMEM((U, NY * W), BF16),
            pltpu.VMEM((V, NZ * W), BF16),
            pltpu.VMEM((4, V, W), BF16),
            pltpu.VMEM((4, V, W), BF16),
            pltpu.VMEM((V, NZ * W), BF16),
            pltpu.VMEM((4, V, W), BF16),
            pltpu.VMEM((4, V, W), BF16),
            pltpu.VMEM((U, NZ * W), BF16),
            pltpu.VMEM((V, NY * W), BF16),
            pltpu.VMEM((2, V, W), F32),
            pltpu.VMEM((2, 2, V, W), BF16),
            pltpu.VMEM((R, W), F32),
            pltpu.SemaphoreType.DMA,
            pltpu.SemaphoreType.DMA((COPIES,)),
            pltpu.SemaphoreType.DMA((COPIES,)),
        ],
        compiler_params=pltpu.CompilerParams(
            collective_id=0, has_side_effects=True, vmem_limit_bytes=32 << 20
        ),
        name="newton_schulz",
    )(iterate)


def solution(mesh):
    placed = (P("row", "col"),)
    return jax.shard_map(
        body, mesh=mesh, in_specs=placed, out_specs=P("row", "col"), check_vma=False
    )
```

time: 663 us -> 79.3 us (0.12)
  waiting for transfers between devices: 631 us -> 0 us
  Pallas kernels: 0 us -> 77.6 us
  between operations: 13.2 us -> 0.01 us
  matrix products: 11.2 us -> 0 us
    psum x1 -> x0, waiting for transfers between devices: 329 us -> none  [from_root(): return lax.psum(block, axis)]
    all_gather x4 -> x0, waiting for transfers between devices: 300 us -> none  [the longest x1 112 us: body(): first_term = add_rows(lax.all_gather(iterate, 'col', axis=1, tiled=True))]
    pallas_call x0 -> x1, Pallas kernels: none -> 77.6 us  [body(): pl.pallas_call(kernel, out_shape=jax.ShapeDtypeStruct((R, W), BF16), in_s...]
    dot_general x3 -> x0, matrix products: 11.2 us -> none  [the longest x2 7.1 us: add_rows(): return jnp.dot(segment, gram_columns, preferred_element_type=jnp.float32)]
  transfers between devices with their start and end apart: 5 -> 0, of which waited for: 5 -> 0; matrix products, arithmetic and copies ran while one was open for 1% -> 0% of each run, Pallas kernels for 0% -> 0%
where the time goes in v2:
time: 79.3 us; the launch traced here: 79.2 us
  Pallas kernels  77.6 us (98%)
  local copies, waits for them, and re-layouts  1.56 us (2%)
    pallas_call x1, Pallas kernels, body(): pl.pallas_call(kernel, out_shape=jax.ShapeDtypeStruct((R, W), BF16), in_s...  77.6 us

profile of v2, /device:TPU:1, one launch (start us, length us, event | category | flops | bytes accessed | tf_op | source)
XLA Modules:
  0.0 79.2 jit_solution(2424351317682965251)
XLA Ops:
  0.0 0.0 copy-start
  0.0 0.9 %copy-done = bf16[512,128]{1,0:T(8,128)(2,1)S(1)} copy-done((bf16[512,128]{1,0:T(8,128)(2,1)S(1)}, bf16[512,128]{1,0:T(8,128)(2,1)}, u32[]{:S(2)}) %copy-start) | copy-done | bytes 131096
  0.9 77.6 %newton_schulz.1 = bf16[512,128]{1,0:T(8,128)(2,1)S(1)} custom-call(bf16[512,128]{1,0:T(8,128)(2,1)S(1)} %copy-done), custom_call_target="tpu_custom_call" | custom-call | tf_op jit(solution)/shard_map/newton_schulz/pallas_call | solution.py:282
  78.5 0.7 copy.3
Async XLA Ops:
  0.0 0.9 %copy-start = (bf16[512,128]{1,0:T(8,128)(2,1)S(1)}, bf16[512,128]{1,0:T(8,128)(2,1)}, u32[]{:S(2)}) copy-start(bf16[512,128]{1,0:T(8,128)(2,1)} %x_hbm.1) | copy-start | bytes 393220

commit v3 on v2

v3 whole, which is shorter than its diff:
```python
import math

import jax
import jax.numpy as jnp
from jax import lax
from jax.experimental import pallas as pl
from jax.experimental.pallas import tpu as pltpu
from jax.sharding import PartitionSpec as P

MESH = pl.DeviceIdType.MESH
BF16 = jnp.bfloat16
F32 = jnp.float32

R, W = 512, 128
NZ, NY = 8, 4
PARTS = 4
LAG = 1
U_CHUNKS = 4
V_CHUNKS = 4
Z_PLAN = ((0, 2), (0, 1), (2, 3), (2, 4))
SLABS = [(dx, dy) for dx in (2, 1, 3, 0) for dy in (1, 0) if (dx, dy) != (0, 0)]
SCALE = 0.2 * math.sqrt(8192)
ORDER = (0, 1, 7, 2, 6, 3, 5, 4)
PLACE = {d: i for i, d in enumerate(ORDER)}
GRAM_CHUNKS = ((0, 3), (3, 8))


def tdot(left, right):
    return lax.dot_general(left, right, (((0,), (0,)), ((), ())), preferred_element_type=F32)


def kernel(
    x_hbm, o_ref, x_ref, xa, xb, xao, xbo, gp, rb, g, su1, ru1, su2, ru2, ov1, rv1, fv1, ov2, rv2, fv2, ah, av, kept, through, acc,
    load_sem, send_sems, recv_sems,
):
    r, c_ = lax.axis_index("row"), lax.axis_index("col")
    x, yl, q = r // 4, (r // 2) % 2, r % 2
    z, yh = c_ // 4, c_ % 4
    slab = x * 2 + yl
    sibling = (x * 4 + yl * 2 + (1 - q), c_)
    z_dev = {d: (r, ((z + d) % NZ) * 4 + yh) for d in (1, 2, 6, 7)}
    y_dev = {e: (r, z * 4 + (yh + e) % NY) for e in range(1, NY)}
    slab_of, slab_dev, slab_from = {}, {}, {}
    for dx, dy in SLABS:
        tx, ty = (x + dx) % 4, (yl + dy) % 2
        slab_of[dx, dy] = tx * 2 + ty
        slab_dev[dx, dy] = (tx * 4 + ty * 2 + q, c_)
        slab_from[dx, dy] = ((x + 4 - dx) % 4) * 2 + ty

    load = pltpu.make_async_copy(x_hbm, x_ref, load_sem)
    load.start()
    barrier = pltpu.get_barrier_semaphore()
    partners = [sibling] + list(z_dev.values()) + list(y_dev.values()) + list(slab_dev.values())
    for device in partners:
        pl.semaphore_signal(barrier, inc=1, device_id=device, device_id_type=MESH)
    load.wait()
    xa[:, 0:W] = x_ref[...]
    xb[:, 0:W] = x_ref[...]
    pl.semaphore_wait(barrier, len(partners))

    started = []

    def send(src, dst, device):
        at = len(started)
        copy = pltpu.make_async_remote_copy(
            src_ref=src,
            dst_ref=dst,
            send_sem=send_sems.at[at],
            recv_sem=recv_sems.at[at],
            device_id=device,
            device_id_type=MESH,
        )
        copy.start()
        started.append(copy)
        return copy

    settled, mark = [0], [0]

    def settle():
        for copy in started[settled[0] : mark[0]]:
            copy.wait_send()
        settled[0], mark[0] = mark[0], len(started)

    def slot(ref, at, first=0, count=R):
        return ref.at[pl.ds(first, count), pl.ds(at * W, W)]

    def z_near(src, buf, first, count):
        got = {}
        for d in (2, 6, 1, 7):
            got[(NZ - d) % NZ] = send(src, slot(buf, PLACE[(NZ - d) % NZ], first, count), z_dev[d])
        return got

    def z_far(buf, d, first, count, got):
        step = 7 if d == 2 else 1
        twice = 6 if d == 2 else 2
        far = 3 if d == 2 else 5
        here = slot(buf, PLACE[d], first, count)
        got[far] = send(here, slot(buf, PLACE[far], first, count), z_dev[step])
        half = first if d == 2 else first + count // 2
        got[4, d] = send(
            slot(buf, PLACE[d], half, count // 2), slot(buf, PLACE[4], half, count // 2), z_dev[twice]
        )

    z_in, z_seen = {}, set()

    def z_wait(d):
        for key, copy in z_in.items():
            if key[0] == d and key not in z_seen:
                z_seen.add(key)
                copy.wait_recv()

    PART = R // PARTS

    def z_hop(near, target):
        for p in range(PARTS):
            for side in (1, -1):
                key = (near * side % NZ, p)
                if near and key not in z_seen:
                    z_seen.add(key)
                    z_in[key].wait_recv()
                hop = z_dev[-side * (target - near) % NZ]
                rows, key = (p * PART, PART), (target * side % NZ, p)
                if target == 4:
                    rows = (p * PART + (0 if side == 1 else PART // 2), PART // 2)
                    key = (4, p, side)
                src = slot(xa, PLACE[near * side % NZ], *rows) if near else x_ref.at[pl.ds(*rows), :]
                z_in[key] = send(src, slot(xa, PLACE[target * side % NZ], *rows), hop)

    for near, target in Z_PLAN:
        if near == 0:
            z_hop(near, target)
    y_in = {NY - e: send(x_ref, slot(xb, NY - e), y_dev[e]) for e in (2, 1, 3)}
    xa_in = {0: send(x_ref, slot(xao, 0), sibling)}
    xb_in = {0: send(x_ref, slot(xbo, 0), sibling)}

    def pass_xa(d):
        xa_in[d] = send(slot(xa, PLACE[d]), slot(xao, PLACE[d]), sibling)

    for near, target in Z_PLAN:
        if near:
            z_hop(near, target)
    for d in (1, 7, 2, 6):
        z_wait(d)
        pass_xa(d)
    for e in (1, 3, 2):
        y_in[e].wait_recv()
        xb_in[e] = send(slot(xb, e), slot(xbo, e), sibling)
    for e in (0, 1, 3, 2):
        xb_in[e].wait_recv()

    own = pl.ds(pl.multiple_of(q * (2 * W), 2 * W), 2 * W)

    def gram_rows(chunk):
        first, last = GRAM_CHUNKS[chunk]
        for at in range(first, last):
            part = tdot(xa[:, at * W : (at + 1) * W], xb[:, own])
            part += tdot(xao[:, at * W : (at + 1) * W], xbo[:, own])
            gp[at * W : (at + 1) * W, :] = part.astype(BF16)

    def piece(chunk, w):
        first, last = GRAM_CHUNKS[chunk]
        rows = (last - first) * (W // 8)
        return pl.ds(pl.multiple_of(first * W + w * rows, 16), rows)

    def reduce_start(chunk):
        first, last = GRAM_CHUNKS[chunk]
        rows = (last - first) * (W // 8)
        got = []
        for j, d in enumerate(SLABS):
            dst = rb.at[j, pl.ds(first * (W // 8), rows), :]
            got.append((j, send(gp.at[piece(chunk, slab_of[d]), :], dst, slab_dev[d])))
        return got

    def reduce_finish(chunk, got):
        first, last = GRAM_CHUNKS[chunk]
        mine = piece(chunk, slab)
        total = gp[mine, :].astype(F32)
        for j, copy in got:
            copy.wait_recv()
            total += rb[j, first * (W // 8) : last * (W // 8), :].astype(F32)
        g[mine, own] = total.astype(BF16)
        here = g.at[mine, own]
        gather = [(piece(chunk, slab_from[d]), send(here, here, slab_dev[d])) for d in SLABS]
        return gather, [send(here, here, sibling)]

    def gather_finish(gather, both):
        for rows, copy in gather:
            copy.wait_recv()
            here = g.at[rows, own]
            both.append(send(here, here, sibling))

    reduces, gathers = [], []
    for chunk, (first, last) in enumerate(GRAM_CHUNKS):
        for d in ORDER[first:last]:
            if d in (3, 4, 5):
                z_wait(d)
                pass_xa(d)
        for d in ORDER[first:last]:
            xa_in[d].wait_recv()
        gram_rows(chunk)
        reduces.append(reduce_start(chunk))
        if chunk >= LAG:
            gathers.append(reduce_finish(chunk - LAG, reduces[chunk - LAG]))
    settle()
    for chunk in range(len(GRAM_CHUNKS) - LAG, len(GRAM_CHUNKS)):
        gathers.append(reduce_finish(chunk, reduces[chunk]))
    settle()
    for gather, both in gathers:
        gather_finish(gather, both)
    for gather, both in gathers:
        for copy in both:
            copy.wait_recv()

    def u_product(rows_of, rows, out, into):
        first, count = rows
        got = {}
        left = rows_of[first : first + count, :]
        high = jnp.dot(left, g[:, 2 * W :], preferred_element_type=F32).astype(BF16)
        for e in (2, 3):
            out[first : first + count, e * W : (e + 1) * W] = high[:, (e - 2) * W : (e - 1) * W]
            got[NY - e] = send(slot(out, e, *rows), slot(into, NY - e, *rows), y_dev[e])
        low = jnp.dot(left, g[:, : 2 * W], preferred_element_type=F32)
        out[first : first + count, W : 2 * W] = low[:, W:].astype(BF16)
        got[3] = send(slot(out, 1, *rows), slot(into, 3, *rows), y_dev[1])
        return low[:, :W], got

    def u_sum(total, rows, into, got):
        first, count = rows
        for e in (1, 3, 2):
            got[e].wait_recv()
            total += into[first : first + count, e * W : (e + 1) * W].astype(F32)
        return total

    def v_product(left, rows, out, relay, into):
        first, count = rows[0], rows[1]
        part = lax.dot_general(
            left, g[...], (((1,), (1,)), ((), ())), preferred_element_type=F32
        )
        out[first : first + count, :] = part.astype(BF16)
        got = {}
        half = count // 2
        for n, d, start in ((2, 2, first), (3, 6, first + half)):
            src = slot(out, PLACE[4], start, half)
            got[n] = send(src, relay.at[n, pl.ds(first, half), :], z_dev[d])
        for n, d, far in ((0, 1, 3), (1, 7, 5)):
            src = slot(out, PLACE[far], first, count)
            got[n] = send(src, relay.at[n, pl.ds(first, count), :], z_dev[d])
        near = []
        for n, d in ((0, 1), (1, 7)):
            src = slot(out, PLACE[d], first, count)
            near.append(send(src, into.at[n, pl.ds(first, count), :], z_dev[d]))
        for n, d in ((0, 2), (1, 6)):
            kept[n, first : first + count] = part[:, PLACE[d] * W : (PLACE[d] + 1) * W]
        return part[:, :W], got, near

    def v_relay(stage, rows, relay, into, got, near):
        first, count = rows[0], rows[1]
        half = count // 2
        top, low = slice(first, first + half), slice(first + half, first + count)
        for n, d in ((0, 2), (1, 6)):
            got[n].wait_recv()
            got[n + 2].wait_recv()
            more = relay[n + 2, top, :].astype(F32)
            for part in (top, low):
                total = kept[n, part] + relay[n, part, :].astype(F32)
                if (part is top) == (n == 0):
                    total += more
                through[stage, n, part] = total.astype(BF16)
            src = through.at[stage, n, pl.ds(first, count), :]
            near.append(send(src, into.at[n + 2, pl.ds(first, count), :], z_dev[d]))

    def v_sum(total, rows, into, near):
        first, count = rows[0], rows[1]
        for n, copy in enumerate(near):
            copy.wait_recv()
            total += into[n, first : first + count, :].astype(F32)
        return total

    def of(rows):
        return slice(rows[0], rows[0] + rows[1])

    def mix(rows, first):
        return 3.4445 * x_ref[of(rows), :].astype(F32) - 4.775 * first

    def chunks(start, count, number):
        return [(start + n * (count // number), count // number) for n in range(number)]

    state = settled[0], mark[0], list(started)

    @pl.when(q == 0)
    def _():
        us = chunks(0, R, U_CHUNKS)
        u_in, ah_in = {}, {}
        for rows in us:
            acc[of(rows), :], u_in[rows] = u_product(xa, rows, su1, ru1)
        settle()
        for rows in us:
            first = u_sum(acc[of(rows), :], rows, ru1, u_in[rows])
            ah[of(rows), 0:W] = first.astype(BF16)
            ah_in[rows] = z_near(slot(ah, 0, *rows), ah, *rows)
            acc[of(rows), :] = mix(rows, first)
        settle()
        for rows in us:
            for d in (2, 6):
                ah_in[rows][d].wait_recv()
                z_far(ah, d, *rows, ah_in[rows])
        for rows in us:
            for d in (1, 7, 3, 5, (4, 2), (4, 6)):
                ah_in[rows][d].wait_recv()
            own_term, u_in[rows] = u_product(ah, rows, su2, ru2)
            acc[of(rows), :] += 2.0315 * own_term
        settle()
        for rows in us:
            second = u_sum(jnp.zeros((rows[1], W), F32), rows, ru2, u_in[rows])
            o_ref[of(rows), :] = (SCALE * (acc[of(rows), :] + 2.0315 * second)).astype(BF16)
        settle()
        settle()

    settled[0], mark[0] = state[:2]
    started[:] = state[2]

    @pl.when(q == 1)
    def _():
        vs = chunks(0, R, V_CHUNKS)
        v_in, av_in = {}, {}
        for rows in vs:
            acc[of(rows), :], *v_in[rows] = v_product(xb[of(rows), :], rows, ov1, rv1, fv1)
        settle()
        for rows in vs:
            v_relay(0, rows, rv1, fv1, *v_in[rows])
        for rows in vs:
            first = v_sum(acc[of(rows), :], rows, fv1, v_in[rows][1])
            av[of(rows), 0:W] = first.astype(BF16)
            av_in[rows] = [
                send(slot(av, 0, *rows), slot(av, NY - e, *rows), y_dev[e]) for e in (2, 1, 3)
            ]
            acc[of(rows), :] = mix(rows, first)
        settle()
        for rows in vs:
            for copy in av_in[rows]:
                copy.wait_recv()
            own_term, *v_in[rows] = v_product(av[of(rows), :], rows, ov2, rv2, fv2)
            acc[of(rows), :] += 2.0315 * own_term
        settle()
        for rows in vs:
            v_relay(1, rows, rv2, fv2, *v_in[rows])
        for rows in vs:
            second = v_sum(jnp.zeros((rows[1], W), F32), rows, fv2, v_in[rows][1])
            o_ref[of(rows), :] = (SCALE * (acc[of(rows), :] + 2.0315 * second)).astype(BF16)
        settle()
        settle()


COPIES = 192


def body(iterate):
    return pl.pallas_call(
        kernel,
        out_shape=jax.ShapeDtypeStruct((R, W), BF16),
        in_specs=[pl.BlockSpec(memory_space=pl.ANY)],
        out_specs=pl.BlockSpec(memory_space=pltpu.VMEM),
        scratch_shapes=[
            pltpu.VMEM((R, W), BF16),
            pltpu.VMEM((R, NZ * W), BF16),
            pltpu.VMEM((R, NY * W), BF16),
            pltpu.VMEM((R, NZ * W), BF16),
            pltpu.VMEM((R, NY * W), BF16),
            pltpu.VMEM((NZ * W, 2 * W), BF16),
            pltpu.VMEM((7, NZ * W // 8, 2 * W), BF16),
            pltpu.VMEM((NZ * W, NY * W), BF16),
            pltpu.VMEM((R, NY * W), BF16),
            pltpu.VMEM((R, NY * W), BF16),
            pltpu.VMEM((R, NY * W), BF16),
            pltpu.VMEM((R, NY * W), BF16),
            pltpu.VMEM((R, NZ * W), BF16),
            pltpu.VMEM((4, R, W), BF16),
            pltpu.VMEM((4, R, W), BF16),
            pltpu.VMEM((R, NZ * W), BF16),
            pltpu.VMEM((4, R, W), BF16),
            pltpu.VMEM((4, R, W), BF16),
            pltpu.VMEM((R, NZ * W), BF16),
            pltpu.VMEM((R, NY * W), BF16),
            pltpu.VMEM((2, R, W), F32),
            pltpu.VMEM((2, 2, R, W), BF16),
            pltpu.VMEM((R, W), F32),
            pltpu.SemaphoreType.DMA,
            pltpu.SemaphoreType.DMA((COPIES,)),
            pltpu.SemaphoreType.DMA((COPIES,)),
        ],
        compiler_params=pltpu.CompilerParams(
            collective_id=0, has_side_effects=True, vmem_limit_bytes=32 << 20
        ),
        name="newton_schulz",
    )(iterate)


def solution(mesh):
    placed = (P("row", "col"),)
    return jax.shard_map(
        body, mesh=mesh, in_specs=placed, out_specs=P("row", "col"), check_vma=False
    )
```

time: 79.3 us -> 77.2 us (0.974)
  Pallas kernels: 77.6 us -> 75.5 us
    pallas_call x1, Pallas kernels: 77.6 us -> 75.5 us  [body(): pl.pallas_call(kernel, out_shape=jax.ShapeDtypeStruct((R, W), BF16), in_s...]
where the time goes in v3:
time: 77.2 us; the launch traced here: 77.1 us
  Pallas kernels  75.5 us (98%)
  local copies, waits for them, and re-layouts  1.56 us (2%)
    pallas_call x1, Pallas kernels, body(): pl.pallas_call(kernel, out_shape=jax.ShapeDtypeStruct((R, W), BF16), in_s...  75.5 us
    unnamed x3, local copies, waits for them, and re-layouts  1.56 us

profile of v3, /device:TPU:1, one launch (start us, length us, event | category | flops | bytes accessed | tf_op | source)
XLA Modules:
  0.0 77.1 jit_solution(1838640957504471115)
XLA Ops:
  0.0 0.0 copy-start
  0.0 0.9 %copy-done = bf16[512,128]{1,0:T(8,128)(2,1)S(1)} copy-done((bf16[512,128]{1,0:T(8,128)(2,1)S(1)}, bf16[512,128]{1,0:T(8,128)(2,1)}, u32[]{:S(2)}) %copy-start) | copy-done | bytes 131096
  0.9 75.5 %newton_schulz.1 = bf16[512,128]{1,0:T(8,128)(2,1)S(1)} custom-call(bf16[512,128]{1,0:T(8,128)(2,1)S(1)} %copy-done), custom_call_target="tpu_custom_call" | custom-call | tf_op jit(solution)/shard_map/newton_schulz/pallas_call | solution.py:358
  76.4 0.7 copy.3
Async XLA Ops:
  0.0 0.9 %copy-start = (bf16[512,128]{1,0:T(8,128)(2,1)S(1)}, bf16[512,128]{1,0:T(8,128)(2,1)}, u32[]{:S(2)}) copy-start(bf16[512,128]{1,0:T(8,128)(2,1)} %x_hbm.1) | copy-start | bytes 393220

commit v4 on v3

--- a/solution.py
+++ b/solution.py
@@ -22,7 +22,7 @@
 SCALE = 0.2 * math.sqrt(8192)
 ORDER = (0, 1, 7, 2, 6, 3, 5, 4)
 PLACE = {d: i for i, d in enumerate(ORDER)}
-GRAM_CHUNKS = ((0, 3), (3, 8))
+GRAM_CHUNKS = ((0, 5), (5, 8))
 
 
 def tdot(left, right):

time: 77.2 us -> 76 us (0.984)
  Pallas kernels: 75.5 us -> 74.3 us
    pallas_call x1, Pallas kernels: 75.5 us -> 74.3 us  [body(): pl.pallas_call(kernel, out_shape=jax.ShapeDtypeStruct((R, W), BF16), in_s...]
where the time goes in v4:
time: 76 us; the launch traced here: 75.9 us
  Pallas kernels  74.3 us (98%)
  local copies, waits for them, and re-layouts  1.56 us (2%)
    pallas_call x1, Pallas kernels, body(): pl.pallas_call(kernel, out_shape=jax.ShapeDtypeStruct((R, W), BF16), in_s...  74.3 us
    unnamed x3, local copies, waits for them, and re-layouts  1.56 us

profile of v4, /device:TPU:1, one launch (start us, length us, event | category | flops | bytes accessed | tf_op | source)
XLA Modules:
  0.0 75.9 jit_solution(7876773062133953054)
XLA Ops:
  0.0 0.0 copy-start
  0.0 0.9 %copy-done = bf16[512,128]{1,0:T(8,128)(2,1)S(1)} copy-done((bf16[512,128]{1,0:T(8,128)(2,1)S(1)}, bf16[512,128]{1,0:T(8,128)(2,1)}, u32[]{:S(2)}) %copy-start) | copy-done | bytes 131096
  0.9 74.3 %newton_schulz.1 = bf16[512,128]{1,0:T(8,128)(2,1)S(1)} custom-call(bf16[512,128]{1,0:T(8,128)(2,1)S(1)} %copy-done), custom_call_target="tpu_custom_call" | custom-call | tf_op jit(solution)/shard_map/newton_schulz/pallas_call | solution.py:358
  75.3 0.7 copy.3
Async XLA Ops:
  0.0 0.9 %copy-start = (bf16[512,128]{1,0:T(8,128)(2,1)S(1)}, bf16[512,128]{1,0:T(8,128)(2,1)}, u32[]{:S(2)}) copy-start(bf16[512,128]{1,0:T(8,128)(2,1)} %x_hbm.1) | copy-start | bytes 393220

commit v5 on v4

--- a/solution.py
+++ b/solution.py
@@ -233,10 +233,14 @@
 
     def v_product(left, rows, out, relay, into):
         first, count = rows[0], rows[1]
-        part = lax.dot_general(
-            left, g[...], (((1,), (1,)), ((), ())), preferred_element_type=F32
-        )
-        out[first : first + count, :] = part.astype(BF16)
+        def columns(begin, end):
+            part = lax.dot_general(
+                left, g[begin:end, :], (((1,), (1,)), ((), ())), preferred_element_type=F32
+            )
+            out[first : first + count, begin:end] = part.astype(BF16)
+            return part
+
+        columns(5 * W, NZ * W)
         got = {}
         half = count // 2
         for n, d, start in ((2, 2, first), (3, 6, first + half)):
@@ -245,6 +249,7 @@
         for n, d, far in ((0, 1, 3), (1, 7, 5)):
             src = slot(out, PLACE[far], first, count)
             got[n] = send(src, relay.at[n, pl.ds(first, count), :], z_dev[d])
+        part = columns(0, 5 * W)
         near = []
         for n, d in ((0, 1), (1, 7)):
             src = slot(out, PLACE[d], first, count)

time: 76 us -> 75.6 us (level)
  no operation moved by 1% of the time
where the time goes in v5:
time: 75.6 us; the launch traced here: 75.5 us
  Pallas kernels  73.9 us (98%)
  local copies, waits for them, and re-layouts  1.56 us (2%)
    pallas_call x1, Pallas kernels, body(): pl.pallas_call(kernel, out_shape=jax.ShapeDtypeStruct((R, W), BF16), in_s...  73.9 us
    unnamed x3, local copies, waits for them, and re-layouts  1.56 us

profile of v5, /device:TPU:1, one launch (start us, length us, event | category | flops | bytes accessed | tf_op | source)
XLA Modules:
  0.0 75.5 jit_solution(12706468096673048389)
XLA Ops:
  0.0 0.0 copy-start
  0.0 0.9 %copy-done = bf16[512,128]{1,0:T(8,128)(2,1)S(1)} copy-done((bf16[512,128]{1,0:T(8,128)(2,1)S(1)}, bf16[512,128]{1,0:T(8,128)(2,1)}, u32[]{:S(2)}) %copy-start) | copy-done | bytes 131096
  0.9 73.9 %newton_schulz.1 = bf16[512,128]{1,0:T(8,128)(2,1)S(1)} custom-call(bf16[512,128]{1,0:T(8,128)(2,1)S(1)} %copy-done), custom_call_target="tpu_custom_call" | custom-call | tf_op jit(solution)/shard_map/newton_schulz/pallas_call | solution.py:363
  74.8 0.7 copy.3
Async XLA Ops:
  0.0 0.9 %copy-start = (bf16[512,128]{1,0:T(8,128)(2,1)S(1)}, bf16[512,128]{1,0:T(8,128)(2,1)}, u32[]{:S(2)}) copy-start(bf16[512,128]{1,0:T(8,128)(2,1)} %x_hbm.1) | copy-start | bytes 393220
